TPU v7x, 32 devices: a whole 2x2x4 slice. The times are simulated.
32 devices in a mesh: blk: 8 (over z, y), seq: 4 (over x, core).
Axes of the slice: x: 2, y: 2, z: 4, core: 2. Of those that a mesh axis runs over, the one named last changes fastest.
Arguments:
- tokens: bfloat16 [3072, 4096], P('seq', 'blk'), may hold values from -6 to 6
- grad_out: bfloat16 [3072, 4096], P('seq', 'blk'), may hold values from -0.109375 to 0.109375
- input_weight_blocks: bfloat16 [1024, 128, 128], P('blk'), may hold values from -0.25 to 0.25
- output_weight_blocks: bfloat16 [1024, 128, 128], P('blk'), may hold values from -0.25 to 0.25
- row_ids: int32 [1024], P('blk'), may hold values from 0 to 31, as said below
- lengths: int32 [4], P('seq'), may hold values from 1 to 768, 1920 in all
Outputs:
- grad_in: bfloat16 [1024, 128, 128], P('blk', 'seq')
- grad_w_out: bfloat16 [1024, 128, 128], P('blk', 'seq')
Inputs may be any that keep to these rules, and one draw needn't show every extreme that they name: `row_ids`: the 4 blocks of each hidden column block have distinct row blocks. `lengths`: some window is full.
All inputs are finite; a program needn't handle non-finite values. No bound on the sum of `lengths` on one device may be relied on, other than what follows from the above.
Results may differ from a plain program's by a relative error of at most 0.015.
Values may be sent and summed in bfloat16 or wider, within the bound.
A program may use at most 128 MiB of HBM per device.

v0:
```python
import jax
import jax.numpy as jnp
from jax import lax
from jax.sharding import PartitionSpec as P

BLOCK_SIDE = 128
BLOCKS_PER_COLUMN = 4


gelu_scale = 0.7978845608


def gelu_pair(pre_act):
    tanh_val = jnp.tanh(gelu_scale * (pre_act + 0.044715 * pre_act * pre_act * pre_act))
    activation = 0.5 * pre_act * (1.0 + tanh_val)
    gelu_slope = 0.5 * (1.0 + tanh_val) + 0.5 * pre_act * (
        1.0 - tanh_val * tanh_val
    ) * gelu_scale * (1.0 + 0.134145 * pre_act * pre_act)
    return (activation, gelu_slope)


def shards(tokens, grad_out, input_weight_blocks, output_weight_blocks, row_ids, lengths):
    tok_rows = tokens.shape[0]
    groups = input_weight_blocks.shape[0] // BLOCKS_PER_COLUMN
    live_rows = lax.iota(jnp.int32, tok_rows)[:, None] < lengths[0]
    masked = jnp.where(live_rows, grad_out, jnp.zeros_like(grad_out))
    features = lax.all_gather(tokens, "blk", axis=1, tiled=True)
    x_slots = features.reshape(tok_rows, -1, BLOCK_SIDE)[:, row_ids, :]
    pre_slot = jnp.einsum(
        "tkc,kch->tkh", x_slots, input_weight_blocks, preferred_element_type=jnp.float32
    )
    pre_act = pre_slot.reshape(tok_rows, groups, BLOCKS_PER_COLUMN, BLOCK_SIDE).sum(2)
    activation, gelu_slope = gelu_pair(pre_act)
    activation = activation.astype(jnp.bfloat16)
    gradient = lax.all_gather(masked, "blk", axis=1, tiled=True)
    gradient_slots = gradient.reshape(tok_rows, -1, BLOCK_SIDE)[:, row_ids, :]
    g_four = gradient_slots.reshape(tok_rows, groups, BLOCKS_PER_COLUMN, BLOCK_SIDE)
    output_share = jnp.einsum(
        "tgh,tgrf->grhf", activation, g_four, preferred_element_type=jnp.float32
    )
    output_share = output_share.reshape(-1, BLOCK_SIDE, BLOCK_SIDE)
    slot_gradient = jnp.einsum(
        "xcn,cpn->xcp", gradient_slots, output_weight_blocks, preferred_element_type=jnp.float32
    )
    grad_act = slot_gradient.reshape(tok_rows, groups, BLOCKS_PER_COLUMN, BLOCK_SIDE).sum(2)
    grad_pre = (grad_act * gelu_slope).astype(jnp.bfloat16)
    x_four = x_slots.reshape(tok_rows, groups, BLOCKS_PER_COLUMN, BLOCK_SIDE)
    input_share = jnp.einsum("tgrc,tgh->grch", x_four, grad_pre, preferred_element_type=jnp.float32)
    input_share = input_share.reshape(-1, BLOCK_SIDE, BLOCK_SIDE)
    in_total, out_total = (
        lax.psum_scatter(
            input_share.astype(jnp.bfloat16), "seq", scatter_dimension=1, tiled=True
        ).astype(jnp.float32),
        lax.psum_scatter(
            output_share.astype(jnp.bfloat16), "seq", scatter_dimension=1, tiled=True
        ).astype(jnp.float32),
    )
    return (in_total.astype(jnp.bfloat16), out_total.astype(jnp.bfloat16))


def solution(mesh):
    return jax.shard_map(
        shards,
        mesh=mesh,
        in_specs=(
            P("seq", "blk"),
            P("seq", "blk"),
            P("blk", None, None),
            P("blk", None, None),
            P("blk"),
            P("seq"),
        ),
        out_specs=(P("blk", "seq", None), P("blk", "seq", None)),
        check_vma=False,
    )
```

profile of v0, /device:TPU:0, one launch (start us, length us, event | category | flops | bytes accessed | tf_op | source)
XLA Modules:
  0.0 407.1 jit_solution(17568497418551391394)
XLA Ops:
  7.2 0.0 all-gather.3.cloned.1.call-start
  7.2 2.3 copy.14
  9.5 0.0 all-gather.3.cloned.1.call-update
  9.5 0.0 all-gather.5.cloned.1.call-start
  10.2 1.4 copy.16
  11.6 0.9 broadcast_select_fusion
  12.6 0.0 all-gather.5.cloned.1.call-update
  12.6 0.0 reduce-scatter.3.cloned.1.call-start
  12.7 0.7 compare_select_fusion
  13.3 99.2 %all-gather.3.cloned.1.call-done = bf16[768,4096]{0,1:T(8,128)(2,1)} async-done(((bf16[768,512]{0,1:T(8,128)(2,1)}), bf16[768,4096]{0,1:T(8,128)(2,1)}) %all-gather.3.cloned.1.call-update) | async-done | bytes 6291472 | tf_op jit(solution)/shard_map/all_gather | solution.py:27
  112.5 8.6 %copy.15 = bf16[768,32,128]{2,0,1:T(8,128)(2,1)} copy(bf16[768,32,128]{0,2,1:T(8,128)(2,1)} %bitcast.50) | data formatting | bytes 12582912 | tf_op jit(solution)/shard_map/reshape | solution.py:28
  121.1 91.4 %all-gather.5.cloned.1.call-done = bf16[768,4096]{0,1:T(8,128)(2,1)} async-done(((bf16[768,512]{0,1:T(8,128)(2,1)}), bf16[768,4096]{0,1:T(8,128)(2,1)}) %all-gather.5.cloned.1.call-update) | async-done | bytes 6291472 | tf_op jit(solution)/shard_map/all_gather | solution.py:35
  212.5 8.6 %copy.17 = bf16[768,32,128]{2,0,1:T(8,128)(2,1)} copy(bf16[768,32,128]{0,2,1:T(8,128)(2,1)} %bitcast.51) | data formatting | bytes 12582912 | tf_op jit(solution)/shard_map/reshape | solution.py:36
  221.1 13.8 %gather_fusion.1 = bf16[128,768,128]{2,1,0:T(8,128)(2,1)} fusion(bf16[768,32,128]{2,0,1:T(8,128)(2,1)} %copy.17, s32[1024]{0:T(1024)S(1)} %pad_clamp_fusion), kind=kCustom, calls=%fused_computation.1 | custom fusion | bytes 50332160 | tf_op jit(solution)/shard_map/gather | solution.py:36
  234.9 13.9 %gather_fusion = bf16[128,768,128]{2,1,0:T(8,128)(2,1)} fusion(bf16[768,32,128]{2,0,1:T(8,128)(2,1)} %copy.15, s32[1024]{0:T(1024)S(1)} %pad_clamp_fusion), kind=kCustom, calls=%fused_computation | custom fusion | bytes 50332160 | tf_op jit(solution)/shard_map/gather | solution.py:28
  248.7 20.3 %bitcast_reduce_fusion.1 = f32[768,32,128]{2,0,1:T(8,128)} fusion(bf16[128,128,128]{2,1,0:T(8,128)(2,1)} %param.9, bf16[128,768,128]{2,1,0:T(8,128)(2,1)} %gather_fusion.1), kind=kOutput, calls=%fused_computation.3 | convolution fusion | flops 3230662656 | bytes 41943040 | tf_op jit(solution)/shard_map/xcn,cpn->xcp/dot_general | solution.py:42
  269.1 18.0 %bitcast_reduce_fusion = f32[768,32,128]{2,0,1:T(8,128)} fusion(bf16[128,128,128]{2,1,0:T(8,128)(2,1)} %param.8, bf16[128,768,128]{2,1,0:T(8,128)(2,1)} %gather_fusion), kind=kOutput, calls=%fused_computation.2 | convolution fusion | flops 3230662656 | bytes 41943040 | tf_op jit(solution)/shard_map/tkc,kch->tkh/dot_general | solution.py:29
  287.1 22.9 %fusion.30 = bf16[32,4,128,128]{3,2,1,0:T(8,128)(2,1)} fusion(bf16[768,32,4,128]{3,0,2,1:T(8,128)(2,1)} %bitcast.49, f32[768,32,128]{2,0,1:T(8,128)} %bitcast_reduce_fusion.1, f32[768,32,128]{2,0,1:T(8,128)} %bitcast_reduce_fusion), kind=kOutput, calls=%fused_computation.30 | convolution fusion | flops 3283091456 | bytes 54525952 | tf_op jit(solution)/shard_map/tgrc,tgh->grch/dot_general | solution.py:48
  310.0 0.0 reduce-scatter.3.cloned.1.call-update
  310.1 0.0 reduce-scatter.5.cloned.1.call-start
  310.1 20.0 %fusion.27 = bf16[32,4,128,128]{3,2,1,0:T(8,128)(2,1)} fusion(bf16[768,32,4,128]{3,0,2,1:T(8,128)(2,1)} %bitcast.48, f32[768,32,128]{2,0,1:T(8,128)} %bitcast_reduce_fusion), kind=kOutput, calls=%fused_computation.29 | convolution fusion | flops 3251634176 | bytes 41943040 | tf_op jit(solution)/shard_map/tgh,tgrf->grhf/dot_general | solution.py:38
  330.1 6.4 %copy.20 = bf16[128,128,128]{2,1,0:T(8,128)(2,1)} copy(bf16[128,128,128]{1,2,0:T(8,128)(2,1)} %bitcast.53) | data formatting | bytes 8388608 | tf_op jit(solution)/shard_map/convert_element_type | solution.py:55
  336.5 0.0 reduce-scatter.5.cloned.1.call-update
  336.5 16.4 %reduce-scatter.3.cloned.1.call-done = bf16[128,32,128]{2,1,0:T(8,128)(2,1)} async-done(((bf16[128,128,128]{2,1,0:T(8,128)(2,1)}), bf16[128,32,128]{2,1,0:T(8,128)(2,1)}) %reduce-scatter.3.cloned.1.call-update) | async-done | bytes 1048592 | tf_op jit(solution)/shard_map/reduce_scatter | solution.py:51
  352.9 47.7 %reduce-scatter.5.cloned.1.call-done = bf16[128,32,128]{2,1,0:T(8,128)(2,1)} async-done(((bf16[128,128,128]{2,1,0:T(8,128)(2,1)}), bf16[128,32,128]{2,1,0:T(8,128)(2,1)}) %reduce-scatter.5.cloned.1.call-update) | async-done | bytes 1048592 | tf_op jit(solution)/shard_map/reduce_scatter | solution.py:54
  (2 shorter events, 0.0 us)
Async XLA Ops:
  7.2 105.3 %all-gather.3.cloned.1.call-start = ((), (), s32[]{:S(2)}) async-start(), calls=%async_computation.2 | async-start | bytes 7077888 | tf_op jit(solution)/shard_map/all_gather | solution.py:27
  9.5 203.0 %all-gather.5.cloned.1.call-start = ((), (), s32[]{:S(2)}) async-start(), calls=%async_computation.3 | async-start | bytes 7077888 | tf_op jit(solution)/shard_map/all_gather | solution.py:35
  12.6 340.3 %reduce-scatter.3.cloned.1.call-start = ((), (), s32[]{:S(2)}) async-start(), calls=%async_computation.4 | async-start | bytes 5242880 | tf_op jit(solution)/shard_map/reduce_scatter | solution.py:51
  310.1 90.5 %reduce-scatter.5.cloned.1.call-start = ((), (), s32[]{:S(2)}) async-start(), calls=%async_computation.5 | async-start | bytes 5242880 | tf_op jit(solution)/shard_map/reduce_scatter | solution.py:54
Sparse Core Ops, SparseCore 0:
  10.8 101.7 all-gather.2
  115.3 97.1 all-gather.4
  310.2 42.6 reduce-scatter.2
  356.0 44.5 reduce-scatter.4
where the time goes:
time: 408 us; the launch traced here: 407 us
  waiting for transfers between devices  255 us (62%)
  matrix products  81.3 us (20%)
  local copies, waits for them, and re-layouts  54.9 us (13%)
  between operations  14.4 us (4%)
    all_gather x1, waiting for transfers between devices, shards(): features = lax.all_gather(tokens, 'blk', axis=1, tiled=True)  99.2 us
    all_gather x1, waiting for transfers between devices, shards(): gradient = lax.all_gather(masked, 'blk', axis=1, tiled=True)  91.4 us
    reduce_scatter x1, waiting for transfers between devices, shards(): lax.psum_scatter(output_share.astype(jnp.bfloat16), 'seq', scatter_dimens...  47.7 us
    dot_general x1, matrix products, shards(): jnp.einsum('tgrc,tgh->grch', x_four, grad_pre, preferred_element_type=jnp...  22.9 us
    dot_general x1, matrix products, shards(): jnp.einsum('xcn,cpn->xcp', gradient_slots, output_weight_blocks, preferre...  20.3 us
    dot_general x1, matrix products, shards(): jnp.einsum('tgh,tgrf->grhf', activation, g_four, preferred_element_type=j...  20 us
    dot_general x1, matrix products, shards(): jnp.einsum('tkc,kch->tkh', x_slots, input_weight_blocks, preferred_elemen...  18 us
    reduce_scatter x1, waiting for transfers between devices, shards(): lax.psum_scatter(input_share.astype(jnp.bfloat16), 'seq', scatter_dimensi...  16.4 us
  transfers between devices with their start and end apart: 4, of which 4 were waited for; matrix products, arithmetic and copies ran while one was open for 9% of the time, Pallas kernels for 0%

commit v1 on v0

--- a/solution.py
+++ b/solution.py
@@ -1,6 +1,8 @@
 import jax
 import jax.numpy as jnp
 from jax import lax
+from jax.experimental import pallas as pl
+from jax.experimental.pallas import tpu as pltpu
 from jax.sharding import PartitionSpec as P
 
 BLOCK_SIDE = 128
@@ -58,9 +60,332 @@
     return (in_total.astype(jnp.bfloat16), out_total.astype(jnp.bfloat16))
 
 
+PLAN_MESH = (8, 4)
+NZ = 4
+MESH = pl.DeviceIdType.MESH
+
+
+def pack_gather_grad_kernel(
+    tokens_ref, grad_ref, w_in_ref, w_out_ref, ids_ref, len_ref, out_in_ref, out_out_ref,
+    chip, lens, give, got, feat, w_in, w_out, part, from_core, to_x, from_x,
+    load_sem, core_send, core_recv, x_send, x_recv, z_send, z_recv, y_send, y_recv,
+    sum_core_send, sum_core_recv, sum_x_send, sum_x_recv,
+):
+    rows = chip.shape[2]
+    width = chip.shape[3]
+    keep = feat.shape[1]
+    spare = got.shape[1]
+    per = width // BLOCK_SIDE
+    n_rows = feat.shape[0] // 2
+    groups = part.shape[0]
+    pieces = 2 * per
+
+    blk = lax.axis_index("blk")
+    seq = lax.axis_index("seq")
+    z, y = blk // 2, blk % 2
+    x, core = seq // 2, seq % 2
+    core_dev = {"seq": seq + 1 - 2 * core}
+    x_dev = {"seq": seq + 2 - 4 * x}
+    y_dev = {"blk": blk + 1 - 2 * y}
+    up_dev = {"blk": blk + 2}
+    down_dev = {"blk": blk - 2}
+
+    def remote(src, dst, send, recv, device):
+        return pltpu.make_async_remote_copy(
+            src_ref=src, dst_ref=dst, send_sem=send, recv_sem=recv,
+            device_id=device, device_id_type=MESH,
+        )
+
+    barrier = pltpu.get_barrier_semaphore()
+    for device in (core_dev, x_dev, y_dev):
+        pl.semaphore_signal(barrier, inc=1, device_id=device, device_id_type=MESH)
+
+    @pl.when(z > 0)
+    def _():
+        pl.semaphore_signal(barrier, inc=1, device_id=down_dev, device_id_type=MESH)
+
+    @pl.when(z < NZ - 1)
+    def _():
+        pl.semaphore_signal(barrier, inc=1, device_id=up_dev, device_id_type=MESH)
+
+    own_loads = [
+        pltpu.make_async_copy(ref, chip.at[a, core], load_sem.at[a])
+        for a, ref in enumerate((tokens_ref, grad_ref))
+    ]
+    weight_loads = [
+        pltpu.make_async_copy(w_in_ref, w_in, load_sem.at[2]),
+        pltpu.make_async_copy(w_out_ref, w_out, load_sem.at[3]),
+    ]
+    for load in own_loads:
+        load.start()
+    lens[core] = jnp.full(lens.shape[1:], len_ref[0], jnp.int32)
+    pl.semaphore_wait(barrier, 3 + jnp.where(z > 0, 1, 0) + jnp.where(z < NZ - 1, 1, 0))
+
+    len_swap = remote(lens.at[core], lens.at[core], core_send.at[2], core_recv.at[2], core_dev)
+    len_swap.start()
+    swaps = [
+        remote(ref, chip.at[a, core], core_send.at[a], core_recv.at[a], core_dev)
+        for a, ref in enumerate((tokens_ref, grad_ref))
+    ]
+    for swap in swaps:
+        swap.start()
+    for load in weight_loads:
+        load.start()
+    len_swap.wait()
+    len_a = lens[0][0:1, 0:1]
+    len_b = lens[1][0:1, 0:1]
+    count = len_a + len_b
+    row = lax.broadcasted_iota(jnp.int32, (1, 2 * rows), 1)
+    place = jnp.where(
+        row < rows,
+        jnp.where(row < len_a, row, -1),
+        jnp.where(row - rows < len_b, row - rows + len_a, -1),
+    )
+    odd_give = jnp.bitwise_and(4 * keep - count + core, 1)
+    odd_got = jnp.bitwise_and(count + core, 1)
+    keep_at = 2 * lax.broadcasted_iota(jnp.int32, (keep, 1), 0) + core
+    give_at = 2 * keep + odd_give + 2 * lax.broadcasted_iota(jnp.int32, (spare, 1), 0)
+    got_at = count + odd_got + 2 * lax.broadcasted_iota(jnp.int32, (1, spare), 1)
+    one, zero = jnp.float32(1), jnp.float32(0)
+    pick_keep = jnp.where(place == keep_at, one, zero).astype(jnp.bfloat16)
+    pick_give = jnp.where(place == give_at, one, zero).astype(jnp.bfloat16)
+    pick_got = jnp.where(got_at == keep_at, one, zero).astype(jnp.bfloat16)
+
+    def piece_at(a, source, i):
+        return a * n_rows + per * source + i
+
+    def feat_piece(source, p):
+        return feat.at[(p // per) * n_rows + per * source + p % per]
+
+    def z_copy(up, source_z, p, recv_only=False):
+        ref = feat_piece(2 * source_z + y, p)
+        return remote(
+            ref, ref, z_send.at[0 if up else 1, source_z, p], z_recv.at[source_z, p],
+            y_dev if recv_only else (up_dev if up else down_dev),
+        )
+
+    def y_copy(source_z, source_y, p):
+        ref = feat_piece(2 * source_z + source_y, p)
+        return remote(ref, ref, y_send.at[source_z, p], y_recv.at[source_z, p], y_dev)
+
+    def both(a):
+        return chip[a].reshape(2 * rows, width)
+
+    x_moves = []
+    for a in range(2):
+        own_loads[a].wait()
+        swaps[a].wait()
+        give[a] = jnp.dot(pick_give, both(a), preferred_element_type=jnp.float32).astype(jnp.bfloat16)
+        move = remote(give.at[a], got.at[a], x_send.at[a], x_recv.at[a], x_dev)
+        move.start()
+        x_moves.append(move)
+    kept = [jnp.dot(pick_keep, both(a), preferred_element_type=jnp.float32) for a in range(2)]
+    for a in range(2):
+        x_moves[a].wait()
+        block = kept[a] + jnp.dot(pick_got, got[a], preferred_element_type=jnp.float32)
+        block = block.astype(jnp.bfloat16)
+        for i in range(per):
+            feat[piece_at(a, blk, i)] = block[:, i * BLOCK_SIDE : (i + 1) * BLOCK_SIDE]
+
+        def send_own(i, carry):
+            p = a * per + i
+            y_copy(z, y, p).start()
+
+            @pl.when(z < NZ - 1)
+            def _():
+                z_copy(True, z, p).start()
+
+            @pl.when(z > 0)
+            def _():
+                z_copy(False, z, p).start()
+
+            return carry
+
+        lax.fori_loop(0, per, send_own, 0)
+
+    for step in range(NZ - 1):
+
+        def pass_on(p, carry):
+            below = z - 1 - step
+            above = z + 1 + step
+
+            @pl.when(below >= 0)
+            def _():
+                z_copy(True, below, p, recv_only=True).wait_recv()
+                y_copy(below, y, p).start()
+
+                @pl.when(z < NZ - 1)
+                def _():
+                    z_copy(True, below, p).start()
+
+            @pl.when(above < NZ)
+            def _():
+                z_copy(False, above, p, recv_only=True).wait_recv()
+                y_copy(above, y, p).start()
+
+                @pl.when(z > 0)
+                def _():
+                    z_copy(False, above, p).start()
+
+            return carry
+
+        lax.fori_loop(0, pieces, pass_on, 0)
+
+    def end_gather(p, carry):
+        for source_z in range(NZ):
+            y_copy(source_z, 1 - y, p).wait_recv()
+        return carry
+
+    lax.fori_loop(0, pieces, end_gather, 0)
+
+    for load in weight_loads:
+        load.wait()
+
+    def core_sum(g):
+        return remote(part.at[g, 1 - core], from_core.at[g], sum_core_send.at[g], sum_core_recv.at[g], core_dev)
+
+    def x_sum(g):
+        return remote(to_x.at[g], from_x.at[g], sum_x_send.at[g], sum_x_recv.at[g], x_dev)
+
+    def send_sum(g):
+        core_sum(g).wait_recv()
+        total = part[g, core, 1 - x].astype(jnp.float32) + from_core[g, 1 - x].astype(jnp.float32)
+        to_x[g] = total.astype(jnp.bfloat16)
+        x_sum(g).start()
+
+    quarter = BLOCK_SIDE // 4
+
+    def group(g, carry):
+        ids = [ids_ref[BLOCKS_PER_COLUMN * g + i] for i in range(BLOCKS_PER_COLUMN)]
+        x_cat = jnp.concatenate([feat[r] for r in ids], axis=1)
+        g_cat = jnp.concatenate([feat[n_rows + r] for r in ids], axis=1)
+        slots = pl.ds(BLOCKS_PER_COLUMN * g, BLOCKS_PER_COLUMN)
+        w_rows = w_in[slots].reshape(BLOCKS_PER_COLUMN * BLOCK_SIDE, BLOCK_SIDE)
+        wo = w_out[slots]
+        w_cols = jnp.concatenate([wo[i] for i in range(BLOCKS_PER_COLUMN)], axis=1)
+        pre_act = jnp.dot(x_cat, w_rows, preferred_element_type=jnp.float32)
+        grad_act = lax.dot_general(
+            g_cat, w_cols, (((1,), (1,)), ((), ())), preferred_element_type=jnp.float32
+        )
+        activation, gelu_slope = gelu_pair(pre_act)
+        activation = activation.astype(jnp.bfloat16)
+        grad_pre = (grad_act * gelu_slope).astype(jnp.bfloat16)
+        first = (((0,), (0,)), ((), ()))
+        share_in = lax.dot_general(grad_pre, x_cat, first, preferred_element_type=jnp.float32)
+        share_out = lax.dot_general(activation, g_cat, first, preferred_element_type=jnp.float32)
+        for i in range(BLOCKS_PER_COLUMN):
+            cols = slice(i * BLOCK_SIDE, (i + 1) * BLOCK_SIDE)
+            two = (share_in[:, cols].T, share_out[:, cols])
+            for a in range(2):
+                rounded = two[a].astype(jnp.bfloat16)
+                for q in range(4):
+                    part[g, q % 2, q // 2, a, i] = rounded[q * quarter : (q + 1) * quarter]
+        core_sum(g).start()
+
+        @pl.when(g > 0)
+        def _():
+            send_sum(g - 1)
+
+        return carry
+
+    lax.fori_loop(0, groups, group, 0)
+    send_sum(groups - 1)
+
+    def finish(g, carry):
+        x_sum(g).wait_recv()
+        total = (
+            part[g, core, x].astype(jnp.float32)
+            + from_core[g, x].astype(jnp.float32)
+            + from_x[g].astype(jnp.float32)
+        ).astype(jnp.bfloat16)
+        slots = pl.ds(BLOCKS_PER_COLUMN * g, BLOCKS_PER_COLUMN)
+        out_in_ref[slots] = total[0]
+        out_out_ref[slots] = total[1]
+        return carry
+
+    lax.fori_loop(0, groups, finish, 0)
+
+    def end_sums(g, carry):
+        core_sum(g).wait_send()
+        x_sum(g).wait_send()
+        return carry
+
+    lax.fori_loop(0, groups, end_sums, 0)
+
+    def end_sends(p, carry):
+        for source_z in range(NZ):
+            y_copy(source_z, y, p).wait_send()
+
+            @pl.when(jnp.logical_and(z < NZ - 1, source_z <= z))
+            def _():
+                z_copy(True, source_z, p).wait_send()
+
+            @pl.when(jnp.logical_and(z > 0, source_z >= z))
+            def _():
+                z_copy(False, source_z, p).wait_send()
+
+        return carry
+
+    lax.fori_loop(0, pieces, end_sends, 0)
+
+
+def packed_shards(tokens, grad_out, input_weight_blocks, output_weight_blocks, row_ids, lengths):
+    rows, width = tokens.shape
+    slots = input_weight_blocks.shape[0]
+    groups = slots // BLOCKS_PER_COLUMN
+    n_blk, n_seq = PLAN_MESH
+    keep = rows * 5 // 8
+    spare = rows - keep
+    n_rows = n_blk * width // BLOCK_SIDE
+    pieces = 2 * width // BLOCK_SIDE
+    quarter = BLOCK_SIDE // n_seq
+    sums = (2, BLOCKS_PER_COLUMN, quarter, BLOCK_SIDE)
+    bf16 = jnp.bfloat16
+    dma = pltpu.SemaphoreType.DMA
+    any_spec = pl.BlockSpec(memory_space=pl.ANY)
+    smem = pl.BlockSpec(memory_space=pltpu.SMEM)
+    vmem = pl.BlockSpec(memory_space=pltpu.VMEM)
+    out = jax.ShapeDtypeStruct((slots, quarter, BLOCK_SIDE), bf16)
+    return pl.pallas_call(
+        pack_gather_grad_kernel,
+        out_shape=(out, out),
+        in_specs=[any_spec] * 4 + [smem] * 2,
+        out_specs=(vmem, vmem),
+        scratch_shapes=[
+            pltpu.VMEM((2, 2, rows, width), bf16),
+            pltpu.VMEM((2, 8, 128), jnp.int32),
+            pltpu.VMEM((2, spare, width), bf16),
+            pltpu.VMEM((2, spare, width), bf16),
+            pltpu.VMEM((2 * n_rows, keep, BLOCK_SIDE), bf16),
+            pltpu.VMEM((slots, BLOCK_SIDE, BLOCK_SIDE), bf16),
+            pltpu.VMEM((slots, BLOCK_SIDE, BLOCK_SIDE), bf16),
+            pltpu.VMEM((groups, 2, 2) + sums, bf16),
+            pltpu.VMEM((groups, 2) + sums, bf16),
+            pltpu.VMEM((groups,) + sums, bf16),
+            pltpu.VMEM((groups,) + sums, bf16),
+            dma((4,)),
+            dma((3,)),
+            dma((3,)),
+            dma((2,)),
+            dma((2,)),
+            dma((2, NZ, pieces)),
+            dma((NZ, pieces)),
+            dma((NZ, pieces)),
+            dma((NZ, pieces)),
+            dma((groups,)),
+            dma((groups,)),
+            dma((groups,)),
+            dma((groups,)),
+        ],
+        compiler_params=pltpu.CompilerParams(
+            collective_id=0, has_side_effects=True, vmem_limit_bytes=56 * 1024 * 1024
+        ),
+    )(tokens, grad_out, input_weight_blocks, output_weight_blocks, row_ids, lengths)
+
+
 def solution(mesh):
     return jax.shard_map(
-        shards,
+        packed_shards if tuple(mesh.shape.values()) == PLAN_MESH else shards,
         mesh=mesh,
         in_specs=(
             P("seq", "blk"),

time: 408 us -> 162 us (0.40)
  waiting for transfers between devices: 255 us -> 0 us
  Pallas kernels: 0 us -> 156 us
  matrix products: 81.3 us -> 0 us
  local copies, waits for them, and re-layouts: 54.9 us -> 4.52 us
  between operations: 14.4 us -> 1.29 us
    all_gather x2 -> x0, waiting for transfers between devices: 191 us -> none  [the longest x1 99.2 us: shards(): features = lax.all_gather(tokens, 'blk', axis=1, tiled=True)]
    pallas_call x0 -> x1, Pallas kernels: none -> 156 us  [packed_shards(): pl.pallas_call(pack_gather_grad_kernel, out_shape=(out, out), in_specs=[a...]
    dot_general x4 -> x0, matrix products: 81.3 us -> none  [the longest x1 22.9 us: shards(): jnp.einsum('tgrc,tgh->grch', x_four, grad_pre, preferred_element_type=jnp...]
    reduce_scatter x2 -> x0, waiting for transfers between devices: 64 us -> none  [the longest x1 47.7 us: shards(): lax.psum_scatter(output_share.astype(jnp.bfloat16), 'seq', scatter_dimens...]
    gather x2 -> x0, local copies, waits for them, and re-layouts: 27.7 us -> none  [the longest x1 13.9 us: shards(): x_slots = features.reshape(tok_rows, -1, BLOCK_SIDE)[:, row_ids, :]]
    reshape x2 -> x0, local copies, waits for them, and re-layouts: 17.2 us -> none  [the longest x1 8.62 us: shards(): x_slots = features.reshape(tok_rows, -1, BLOCK_SIDE)[:, row_ids, :]]
    convert_element_type x1 -> x0, local copies, waits for them, and re-layouts: 6.38 us -> none  [shards(): output_share.astype(jnp.bfloat16)]
  transfers between devices with their start and end apart: 4 -> 0, of which waited for: 4 -> 0; matrix products, arithmetic and copies ran while one was open for 9% -> 0% of each run, Pallas kernels for 0% -> 0%
where the time goes in v1:
time: 162 us
  Pallas kernels  156 us (96%)
  local copies, waits for them, and re-layouts  4.52 us (3%)
    pallas_call x1, Pallas kernels, packed_shards(): pl.pallas_call(pack_gather_grad_kernel, out_shape=(out, out), in_specs=[a...  156 us
    unnamed x2, local copies, waits for them, and re-layouts  4.52 us

profile of v1, /device:TPU:0, one launch (start us, length us, event | category | flops | bytes accessed | tf_op | source)
XLA Modules:
  0.0 161.9 jit_solution(8618259669028676615)
XLA Ops:
  1.3 156.1 %shard_map.77 = (bf16[128,32,128]{2,1,0:T(8,128)(2,1)}, bf16[128,32,128]{2,1,0:T(8,128)(2,1)}) custom-call(bf16[768,512]{1,0:T(8,128)(2,1)} %tokens_ref.1, bf16[768,512]{1,0:T(8,128)(2,1)} %grad_ref.1, bf16[128,128,128]{2,1,0:T(8,128)(2,1)} %w_in_ref.1, bf16[128,128,128]{2,1,0:T(8,128)(2,1)} %w_out_ref.1, s32[128]{0:T(128)} %ids_ref.1, s32[1]{0:T(128)S(6)} %copy.10.len_ref), custom_call_target="tpu_custom_call" | custom-call | tf_op jit(solution)/shard_map/pallas_call | solution.py:349
  157.4 2.3 %copy.11 = bf16[128,32,128]{2,1,0:T(8,128)(2,1)} copy(bf16[128,32,128]{2,1,0:T(8,128)(2,1)} %get-tuple-element.4) | data formatting | bytes 2097152
  159.6 2.3 %copy.12 = bf16[128,32,128]{2,1,0:T(8,128)(2,1)} copy(bf16[128,32,128]{2,1,0:T(8,128)(2,1)} %get-tuple-element.5) | data formatting | bytes 2097152

commit v2 on v1

--- a/solution.py
+++ b/solution.py
@@ -62,6 +62,8 @@
 
 PLAN_MESH = (8, 4)
 NZ = 4
+ACROSS = 3
+DELIVERY_PARTS = 4
 MESH = pl.DeviceIdType.MESH
 
 
@@ -79,6 +81,7 @@
     n_rows = feat.shape[0] // 2
     groups = part.shape[0]
     pieces = 2 * per
+    early = rows - 2 * spare
 
     blk = lax.axis_index("blk")
     seq = lax.axis_index("seq")
@@ -129,8 +132,6 @@
     ]
     for swap in swaps:
         swap.start()
-    for load in weight_loads:
-        load.start()
     len_swap.wait()
     len_a = lens[0][0:1, 0:1]
     len_b = lens[1][0:1, 0:1]
@@ -147,96 +148,139 @@
     give_at = 2 * keep + odd_give + 2 * lax.broadcasted_iota(jnp.int32, (spare, 1), 0)
     got_at = count + odd_got + 2 * lax.broadcasted_iota(jnp.int32, (1, spare), 1)
     one, zero = jnp.float32(1), jnp.float32(0)
-    pick_keep = jnp.where(place == keep_at, one, zero).astype(jnp.bfloat16)
+    pick_early = jnp.where(place == keep_at[:early], one, zero).astype(jnp.bfloat16)
+    pick_late = jnp.where(place == keep_at[early:], one, zero).astype(jnp.bfloat16)
     pick_give = jnp.where(place == give_at, one, zero).astype(jnp.bfloat16)
-    pick_got = jnp.where(got_at == keep_at, one, zero).astype(jnp.bfloat16)
-
-    def piece_at(a, source, i):
-        return a * n_rows + per * source + i
-
-    def feat_piece(source, p):
-        return feat.at[(p // per) * n_rows + per * source + p % per]
-
-    def z_copy(up, source_z, p, recv_only=False):
-        ref = feat_piece(2 * source_z + y, p)
+    pick_got = jnp.where(got_at == keep_at[early:], one, zero).astype(jnp.bfloat16)
+
+    def feat_piece(source, late, p):
+        at = feat.at[(p // per) * n_rows + per * source + p % per]
+        return at.at[pl.ds(early, keep - early)] if late else at.at[pl.ds(0, early)]
+
+    def z_copy(up, source_z, other, late, p, recv_only=False):
+        ref = feat_piece(2 * source_z + (1 - y if other else y), late, p)
+        slot = p + (2 * pieces if other else pieces if late else 0)
         return remote(
-            ref, ref, z_send.at[0 if up else 1, source_z, p], z_recv.at[source_z, p],
+            ref, ref, z_send.at[0 if up else 1, source_z, slot], z_recv.at[source_z, slot],
             y_dev if recv_only else (up_dev if up else down_dev),
         )
 
-    def y_copy(source_z, source_y, p):
-        ref = feat_piece(2 * source_z + source_y, p)
-        return remote(ref, ref, y_send.at[source_z, p], y_recv.at[source_z, p], y_dev)
+    def y_copy(source_z, source_y, late, p):
+        ref = feat_piece(2 * source_z + source_y, late, p)
+        slot = p + (pieces if late else 0)
+        return remote(ref, ref, y_send.at[source_z, slot], y_recv.at[source_z, slot], y_dev)
+
+    def z_both(other, late, p):
+        @pl.when(z < NZ - 1)
+        def _():
+            z_copy(True, z, other, late, p).start()
+
+        @pl.when(z > 0)
+        def _():
+            z_copy(False, z, other, late, p).start()
+
+    def send_own(late, a):
+        def body(i, carry):
+            p = a * per + i
+            z_both(False, late, p)
+            y_copy(z, y, late, p).start()
+            return carry
+
+        lax.fori_loop(0, per, body, 0)
+
+    def pass_on(step, late):
+        below = z - 1 - step
+        above = z + 1 + step
+
+        def arrivals(other, across):
+            def body(p, carry):
+                @pl.when(below >= 0)
+                def _():
+                    z_copy(True, below, other, late, p, recv_only=True).wait_recv()
+
+                    @pl.when(z < NZ - 1)
+                    def _():
+                        z_copy(True, below, other, late, p).start()
+
+                    if not across:
+                        y_copy(below, y, late, p).start()
+
+                @pl.when(above < NZ)
+                def _():
+                    z_copy(False, above, other, late, p, recv_only=True).wait_recv()
+
+                    @pl.when(z > 0)
+                    def _():
+                        z_copy(False, above, other, late, p).start()
+
+                    if not across:
+                        y_copy(above, y, late, p).start()
+
+                return carry
+
+            return body
+
+        if late:
+            lax.fori_loop(0, pieces, arrivals(False, False), 0)
+        else:
+            lax.fori_loop(0, ACROSS, arrivals(False, True), 0)
+            lax.fori_loop(ACROSS, pieces, arrivals(False, False), 0)
+            lax.fori_loop(0, ACROSS, arrivals(True, True), 0)
 
     def both(a):
         return chip[a].reshape(2 * rows, width)
 
-    x_moves = []
+    def place_block(block, first, a):
+        block = block.astype(jnp.bfloat16)
+        for i in range(per):
+            feat[a * n_rows + per * blk + i, first : first + block.shape[0]] = block[
+                :, i * BLOCK_SIDE : (i + 1) * BLOCK_SIDE
+            ]
+
     for a in range(2):
         own_loads[a].wait()
         swaps[a].wait()
+        place_block(jnp.dot(pick_early, both(a), preferred_element_type=jnp.float32), 0, a)
+        send_own(False, a)
+    for load in weight_loads:
+        load.start()
+    x_moves = []
+    for a in range(2):
         give[a] = jnp.dot(pick_give, both(a), preferred_element_type=jnp.float32).astype(jnp.bfloat16)
         move = remote(give.at[a], got.at[a], x_send.at[a], x_recv.at[a], x_dev)
         move.start()
         x_moves.append(move)
-    kept = [jnp.dot(pick_keep, both(a), preferred_element_type=jnp.float32) for a in range(2)]
+
+    def turn(p, carry):
+        y_copy(z, 1 - y, False, p).wait_recv()
+        z_both(True, False, p)
+        return carry
+
+    lax.fori_loop(0, ACROSS, turn, 0)
+    pass_on(0, False)
     for a in range(2):
+        kept = jnp.dot(pick_late, both(a), preferred_element_type=jnp.float32)
         x_moves[a].wait()
-        block = kept[a] + jnp.dot(pick_got, got[a], preferred_element_type=jnp.float32)
-        block = block.astype(jnp.bfloat16)
-        for i in range(per):
-            feat[piece_at(a, blk, i)] = block[:, i * BLOCK_SIDE : (i + 1) * BLOCK_SIDE]
-
-        def send_own(i, carry):
-            p = a * per + i
-            y_copy(z, y, p).start()
-
-            @pl.when(z < NZ - 1)
-            def _():
-                z_copy(True, z, p).start()
-
-            @pl.when(z > 0)
-            def _():
-                z_copy(False, z, p).start()
-
-            return carry
-
-        lax.fori_loop(0, per, send_own, 0)
-
-    for step in range(NZ - 1):
-
-        def pass_on(p, carry):
-            below = z - 1 - step
-            above = z + 1 + step
-
-            @pl.when(below >= 0)
-            def _():
-                z_copy(True, below, p, recv_only=True).wait_recv()
-                y_copy(below, y, p).start()
-
-                @pl.when(z < NZ - 1)
-                def _():
-                    z_copy(True, below, p).start()
-
-            @pl.when(above < NZ)
-            def _():
-                z_copy(False, above, p, recv_only=True).wait_recv()
-                y_copy(above, y, p).start()
-
-                @pl.when(z > 0)
-                def _():
-                    z_copy(False, above, p).start()
-
-            return carry
-
-        lax.fori_loop(0, pieces, pass_on, 0)
-
-    def end_gather(p, carry):
+        place_block(kept + jnp.dot(pick_got, got[a], preferred_element_type=jnp.float32), early, a)
+        send_own(True, a)
+    pass_on(1, False)
+    pass_on(0, True)
+    pass_on(2, False)
+    pass_on(1, True)
+    pass_on(2, True)
+
+    def end_early(p, carry):
         for source_z in range(NZ):
-            y_copy(source_z, 1 - y, p).wait_recv()
-        return carry
-
-    lax.fori_loop(0, pieces, end_gather, 0)
+            y_copy(source_z, 1 - y, False, p).wait_recv()
+        return carry
+
+    def end_late(p, carry):
+        for source_z in range(NZ):
+            y_copy(source_z, 1 - y, True, p).wait_recv()
+        return carry
+
+    lax.fori_loop(ACROSS, pieces, end_early, 0)
+    lax.fori_loop(0, pieces, end_late, 0)
 
     for load in weight_loads:
         load.wait()
@@ -312,21 +356,46 @@
 
     lax.fori_loop(0, groups, end_sums, 0)
 
-    def end_sends(p, carry):
-        for source_z in range(NZ):
-            y_copy(source_z, y, p).wait_send()
-
-            @pl.when(jnp.logical_and(z < NZ - 1, source_z <= z))
-            def _():
-                z_copy(True, source_z, p).wait_send()
-
-            @pl.when(jnp.logical_and(z > 0, source_z >= z))
-            def _():
-                z_copy(False, source_z, p).wait_send()
-
-        return carry
-
-    lax.fori_loop(0, pieces, end_sends, 0)
+    def end_sends(other, late, across):
+        def body(p, carry):
+            for source_z in range(NZ):
+                if across:
+                    if not other:
+                        @pl.when(source_z == z)
+                        def _():
+                            y_copy(source_z, y, late, p).wait_send()
+                else:
+                    y_copy(source_z, y, late, p).wait_send()
+
+                @pl.when(jnp.logical_and(z < NZ - 1, source_z <= z))
+                def _():
+                    z_copy(True, source_z, other, late, p).wait_send()
+
+                @pl.when(jnp.logical_and(z > 0, source_z >= z))
+                def _():
+                    z_copy(False, source_z, other, late, p).wait_send()
+
+            return carry
+
+        return body
+
+    lax.fori_loop(0, ACROSS, end_sends(False, False, True), 0)
+    lax.fori_loop(ACROSS, pieces, end_sends(False, False, False), 0)
+    lax.fori_loop(0, ACROSS, end_sends(True, False, True), 0)
+    lax.fori_loop(0, pieces, end_sends(False, True, False), 0)
+
+
+def deliver_kernel(in_ref, out_ref, in_final, out_final, sems):
+    copies = []
+    for a, (source, target) in enumerate(((in_ref, in_final), (out_ref, out_final))):
+        step = source.shape[0] // DELIVERY_PARTS
+        for part in range(DELIVERY_PARTS):
+            at = pl.ds(part * step, step)
+            copies.append(pltpu.make_async_copy(source.at[at], target.at[at], sems.at[a, part]))
+    for copy in copies:
+        copy.start()
+    for copy in copies:
+        copy.wait()
 
 
 def packed_shards(tokens, grad_out, input_weight_blocks, output_weight_blocks, row_ids, lengths):
@@ -346,7 +415,7 @@
     smem = pl.BlockSpec(memory_space=pltpu.SMEM)
     vmem = pl.BlockSpec(memory_space=pltpu.VMEM)
     out = jax.ShapeDtypeStruct((slots, quarter, BLOCK_SIDE), bf16)
-    return pl.pallas_call(
+    parts = pl.pallas_call(
         pack_gather_grad_kernel,
         out_shape=(out, out),
         in_specs=[any_spec] * 4 + [smem] * 2,
@@ -368,10 +437,10 @@
             dma((3,)),
             dma((2,)),
             dma((2,)),
-            dma((2, NZ, pieces)),
-            dma((NZ, pieces)),
-            dma((NZ, pieces)),
-            dma((NZ, pieces)),
+            dma((2, NZ, 2 * pieces + ACROSS)),
+            dma((NZ, 2 * pieces + ACROSS)),
+            dma((NZ, 2 * pieces)),
+            dma((NZ, 2 * pieces)),
             dma((groups,)),
             dma((groups,)),
             dma((groups,)),
@@ -381,6 +450,14 @@
             collective_id=0, has_side_effects=True, vmem_limit_bytes=56 * 1024 * 1024
         ),
     )(tokens, grad_out, input_weight_blocks, output_weight_blocks, row_ids, lengths)
+    return pl.pallas_call(
+        deliver_kernel,
+        out_shape=(out, out),
+        in_specs=[any_spec] * 2,
+        out_specs=(any_spec, any_spec),
+        scratch_shapes=[dma((2, DELIVERY_PARTS))],
+        compiler_params=pltpu.CompilerParams(vmem_limit_bytes=60 * 1024 * 1024),
+    )(*parts)
 
 
 def solution(mesh):

time: 162 us -> 208 us (1.28)
  Pallas kernels: 156 us -> 207 us
  local copies, waits for them, and re-layouts: 4.52 us -> 0 us
    pallas_call x0 -> x1, Pallas kernels: none -> 64.7 us  [packed_shards(): pl.pallas_call(deliver_kernel, out_shape=(out, out), in_specs=[any_spec]...]
    pallas_call x1, Pallas kernels: 156 us -> 142 us  [packed_shards(): pl.pallas_call(pack_gather_grad_kernel, out_shape=(out, out), in_specs=[a...]
    unnamed x2 -> x0, local copies, waits for them, and re-layouts: 4.52 us -> none
where the time goes in v2:
time: 208 us
  Pallas kernels  207 us (100%)
    pallas_call x1, Pallas kernels, packed_shards(): pl.pallas_call(pack_gather_grad_kernel, out_shape=(out, out), in_specs=[a...  142 us
    pallas_call x1, Pallas kernels, packed_shards(): pl.pallas_call(deliver_kernel, out_shape=(out, out), in_specs=[any_spec]...  64.7 us

profile of v2, /device:TPU:0, one launch (start us, length us, event | category | flops | bytes accessed | tf_op | source)
XLA Modules:
  0.0 207.8 jit_solution(3507141342110809126)
XLA Ops:
  1.3 141.9 %shard_map.77 = (bf16[128,32,128]{2,1,0:T(8,128)(2,1)}, bf16[128,32,128]{2,1,0:T(8,128)(2,1)}) custom-call(bf16[768,512]{1,0:T(8,128)(2,1)} %tokens_ref.1, bf16[768,512]{1,0:T(8,128)(2,1)} %grad_ref.1, bf16[128,128,128]{2,1,0:T(8,128)(2,1)} %w_in_ref.1, bf16[128,128,128]{2,1,0:T(8,128)(2,1)} %w_out_ref.1, s32[128]{0:T(128)} %ids_ref.1, s32[1]{0:T(128)S(6)} %copy.8.len_ref), custom_call_target="tpu_custom_call" | custom-call | tf_op jit(solution)/shard_map/pallas_call | solution.py:418
  143.1 64.7 %shard_map.78 = (bf16[128,32,128]{2,1,0:T(8,128)(2,1)}, bf16[128,32,128]{2,1,0:T(8,128)(2,1)}) custom-call(bf16[128,32,128]{2,1,0:T(8,128)(2,1)} %get-tuple-element.4.in_ref, bf16[128,32,128]{2,1,0:T(8,128)(2,1)} %get-tuple-element.5.out_ref), custom_call_target="tpu_custom_call" | custom-call | tf_op jit(solution)/shard_map/pallas_call | solution.py:453

commit v3 on v2

--- a/solution.py
+++ b/solution.py
@@ -63,15 +63,16 @@
 PLAN_MESH = (8, 4)
 NZ = 4
 ACROSS = 3
+TOGETHER = 2
 DELIVERY_PARTS = 4
 MESH = pl.DeviceIdType.MESH
 
 
 def pack_gather_grad_kernel(
     tokens_ref, grad_ref, w_in_ref, w_out_ref, ids_ref, len_ref, out_in_ref, out_out_ref,
-    chip, lens, give, got, feat, w_in, w_out, part, from_core, to_x, from_x,
+    chip, lens, give, got, feat, w_in, w_out, part, from_core, to_x, from_x, staged,
     load_sem, core_send, core_recv, x_send, x_recv, z_send, z_recv, y_send, y_recv,
-    sum_core_send, sum_core_recv, sum_x_send, sum_x_recv,
+    sum_core_send, sum_core_recv, sum_x_send, sum_x_recv, store_sem,
 ):
     rows = chip.shape[2]
     width = chip.shape[3]
@@ -79,7 +80,7 @@
     spare = got.shape[1]
     per = width // BLOCK_SIDE
     n_rows = feat.shape[0] // 2
-    groups = part.shape[0]
+    groups = part.shape[1]
     pieces = 2 * per
     early = rows - 2 * spare
 
@@ -285,21 +286,33 @@
     for load in weight_loads:
         load.wait()
 
-    def core_sum(g):
-        return remote(part.at[g, 1 - core], from_core.at[g], sum_core_send.at[g], sum_core_recv.at[g], core_dev)
-
-    def x_sum(g):
-        return remote(to_x.at[g], from_x.at[g], sum_x_send.at[g], sum_x_recv.at[g], x_dev)
-
-    def send_sum(g):
-        core_sum(g).wait_recv()
-        total = part[g, core, 1 - x].astype(jnp.float32) + from_core[g, 1 - x].astype(jnp.float32)
-        to_x[g] = total.astype(jnp.bfloat16)
-        x_sum(g).start()
+    turns = groups // TOGETHER
+
+    def span(t):
+        return pl.ds(TOGETHER * t, TOGETHER)
+
+    def core_sum(t):
+        return remote(
+            part.at[1 - core, span(t)], from_core.at[span(t)],
+            sum_core_send.at[t], sum_core_recv.at[t], core_dev,
+        )
+
+    def x_sum(t):
+        return remote(
+            to_x.at[span(t)], from_x.at[span(t)], sum_x_send.at[t], sum_x_recv.at[t], x_dev
+        )
+
+    def send_sum(t):
+        core_sum(t).wait_recv()
+        total = part[core, span(t), 1 - x].astype(jnp.float32)
+        total = total + from_core[span(t), 1 - x].astype(jnp.float32)
+        to_x[span(t)] = total.astype(jnp.bfloat16)
+        x_sum(t).start()
 
     quarter = BLOCK_SIDE // 4
-
-    def group(g, carry):
+    first = (((0,), (0,)), ((), ()))
+
+    def column_inputs(g):
         ids = [ids_ref[BLOCKS_PER_COLUMN * g + i] for i in range(BLOCKS_PER_COLUMN)]
         x_cat = jnp.concatenate([feat[r] for r in ids], axis=1)
         g_cat = jnp.concatenate([feat[n_rows + r] for r in ids], axis=1)
@@ -311,50 +324,73 @@
         grad_act = lax.dot_general(
             g_cat, w_cols, (((1,), (1,)), ((), ())), preferred_element_type=jnp.float32
         )
+        return x_cat, g_cat, pre_act, grad_act
+
+    def column_grads(g, x_cat, g_cat, pre_act, grad_act):
         activation, gelu_slope = gelu_pair(pre_act)
         activation = activation.astype(jnp.bfloat16)
         grad_pre = (grad_act * gelu_slope).astype(jnp.bfloat16)
-        first = (((0,), (0,)), ((), ()))
         share_in = lax.dot_general(grad_pre, x_cat, first, preferred_element_type=jnp.float32)
         share_out = lax.dot_general(activation, g_cat, first, preferred_element_type=jnp.float32)
+        share_in = share_in.astype(jnp.bfloat16)
+        share_out = share_out.astype(jnp.bfloat16)
         for i in range(BLOCKS_PER_COLUMN):
             cols = slice(i * BLOCK_SIDE, (i + 1) * BLOCK_SIDE)
             two = (share_in[:, cols].T, share_out[:, cols])
             for a in range(2):
-                rounded = two[a].astype(jnp.bfloat16)
                 for q in range(4):
-                    part[g, q % 2, q // 2, a, i] = rounded[q * quarter : (q + 1) * quarter]
-        core_sum(g).start()
-
-        @pl.when(g > 0)
+                    part[q % 2, g, q // 2, a, i] = two[a][q * quarter : (q + 1) * quarter]
+
+    def turn_columns(t, carry):
+        columns = [TOGETHER * t + u for u in range(TOGETHER)]
+        held = [column_inputs(g) for g in columns]
+        for g, values in zip(columns, held):
+            column_grads(g, *values)
+        core_sum(t).start()
+
+        @pl.when(t > 0)
         def _():
-            send_sum(g - 1)
+            send_sum(t - 1)
 
         return carry
 
-    lax.fori_loop(0, groups, group, 0)
-    send_sum(groups - 1)
-
-    def finish(g, carry):
-        x_sum(g).wait_recv()
+    lax.fori_loop(0, turns, turn_columns, 0)
+    send_sum(turns - 1)
+
+    per_turn = TOGETHER * BLOCKS_PER_COLUMN
+
+    def stores(t):
+        at = pl.ds(per_turn * t, per_turn)
+        return [
+            pltpu.make_async_copy(staged.at[a, at], ref.at[at], store_sem.at[a, t])
+            for a, ref in enumerate((out_in_ref, out_out_ref))
+        ]
+
+    def finish(t, carry):
+        x_sum(t).wait_recv()
         total = (
-            part[g, core, x].astype(jnp.float32)
-            + from_core[g, x].astype(jnp.float32)
-            + from_x[g].astype(jnp.float32)
+            part[core, span(t), x].astype(jnp.float32)
+            + from_core[span(t), x].astype(jnp.float32)
+            + from_x[span(t)].astype(jnp.float32)
         ).astype(jnp.bfloat16)
-        slots = pl.ds(BLOCKS_PER_COLUMN * g, BLOCKS_PER_COLUMN)
-        out_in_ref[slots] = total[0]
-        out_out_ref[slots] = total[1]
+        for u in range(TOGETHER):
+            at = pl.ds(per_turn * t + u * BLOCKS_PER_COLUMN, BLOCKS_PER_COLUMN)
+            for a in range(2):
+                staged[a, at] = total[u, a]
+        for store in stores(t):
+            store.start()
         return carry
 
-    lax.fori_loop(0, groups, finish, 0)
-
-    def end_sums(g, carry):
-        core_sum(g).wait_send()
-        x_sum(g).wait_send()
+    lax.fori_loop(0, turns, finish, 0)
+
+    def end_sums(t, carry):
+        core_sum(t).wait_send()
+        x_sum(t).wait_send()
+        for store in stores(t):
+            store.wait()
         return carry
 
-    lax.fori_loop(0, groups, end_sums, 0)
+    lax.fori_loop(0, turns, end_sums, 0)
 
     def end_sends(other, late, across):
         def body(p, carry):
@@ -385,17 +421,23 @@
     lax.fori_loop(0, pieces, end_sends(False, True, False), 0)
 
 
-def deliver_kernel(in_ref, out_ref, in_final, out_final, sems):
-    copies = []
+def deliver_kernel(in_ref, out_ref, in_final, out_final, held, sems):
+    pairs = []
     for a, (source, target) in enumerate(((in_ref, in_final), (out_ref, out_final))):
         step = source.shape[0] // DELIVERY_PARTS
-        for part in range(DELIVERY_PARTS):
-            at = pl.ds(part * step, step)
-            copies.append(pltpu.make_async_copy(source.at[at], target.at[at], sems.at[a, part]))
-    for copy in copies:
-        copy.start()
-    for copy in copies:
-        copy.wait()
+        for k in range(DELIVERY_PARTS):
+            at = pl.ds(k * step, step)
+            pairs.append((
+                pltpu.make_async_copy(source.at[at], held.at[a, at], sems.at[0, a, k]),
+                pltpu.make_async_copy(held.at[a, at], target.at[at], sems.at[1, a, k]),
+            ))
+    for load, store in pairs:
+        load.start()
+    for load, store in pairs:
+        load.wait()
+        store.start()
+    for load, store in pairs:
+        store.wait()
 
 
 def packed_shards(tokens, grad_out, input_weight_blocks, output_weight_blocks, row_ids, lengths):
@@ -413,13 +455,12 @@
     dma = pltpu.SemaphoreType.DMA
     any_spec = pl.BlockSpec(memory_space=pl.ANY)
     smem = pl.BlockSpec(memory_space=pltpu.SMEM)
-    vmem = pl.BlockSpec(memory_space=pltpu.VMEM)
     out = jax.ShapeDtypeStruct((slots, quarter, BLOCK_SIDE), bf16)
     parts = pl.pallas_call(
         pack_gather_grad_kernel,
         out_shape=(out, out),
         in_specs=[any_spec] * 4 + [smem] * 2,
-        out_specs=(vmem, vmem),
+        out_specs=(any_spec, any_spec),
         scratch_shapes=[
             pltpu.VMEM((2, 2, rows, width), bf16),
             pltpu.VMEM((2, 8, 128), jnp.int32),
@@ -428,10 +469,11 @@
             pltpu.VMEM((2 * n_rows, keep, BLOCK_SIDE), bf16),
             pltpu.VMEM((slots, BLOCK_SIDE, BLOCK_SIDE), bf16),
             pltpu.VMEM((slots, BLOCK_SIDE, BLOCK_SIDE), bf16),
-            pltpu.VMEM((groups, 2, 2) + sums, bf16),
+            pltpu.VMEM((2, groups, 2) + sums, bf16),
             pltpu.VMEM((groups, 2) + sums, bf16),
             pltpu.VMEM((groups,) + sums, bf16),
             pltpu.VMEM((groups,) + sums, bf16),
+            pltpu.VMEM((2, slots, quarter, BLOCK_SIDE), bf16),
             dma((4,)),
             dma((3,)),
             dma((3,)),
@@ -441,10 +483,11 @@
             dma((NZ, 2 * pieces + ACROSS)),
             dma((NZ, 2 * pieces)),
             dma((NZ, 2 * pieces)),
-            dma((groups,)),
-            dma((groups,)),
-            dma((groups,)),
-            dma((groups,)),
+            dma((groups // TOGETHER,)),
+            dma((groups // TOGETHER,)),
+            dma((groups // TOGETHER,)),
+            dma((groups // TOGETHER,)),
+            dma((2, groups // TOGETHER)),
         ],
         compiler_params=pltpu.CompilerParams(
             collective_id=0, has_side_effects=True, vmem_limit_bytes=56 * 1024 * 1024
@@ -455,7 +498,10 @@
         out_shape=(out, out),
         in_specs=[any_spec] * 2,
         out_specs=(any_spec, any_spec),
-        scratch_shapes=[dma((2, DELIVERY_PARTS))],
+        scratch_shapes=[
+            pltpu.VMEM((2, slots, quarter, BLOCK_SIDE), bf16),
+            dma((2, 2, DELIVERY_PARTS)),
+        ],
         compiler_params=pltpu.CompilerParams(vmem_limit_bytes=60 * 1024 * 1024),
     )(*parts)
 

time: 208 us -> 145 us (0.70)
  Pallas kernels: 207 us -> 143 us
    pallas_call x1, Pallas kernels: 64.7 us -> 2.4 us  [packed_shards(): pl.pallas_call(deliver_kernel, out_shape=(out, out), in_specs=[any_spec]...]
where the time goes in v3:
time: 145 us
  Pallas kernels  143 us (99%)
    pallas_call x1, Pallas kernels, packed_shards(): pl.pallas_call(pack_gather_grad_kernel, out_shape=(out, out), in_specs=[a...  141 us

profile of v3, /device:TPU:0, one launch (start us, length us, event | category | flops | bytes accessed | tf_op | source)
XLA Modules:
  0.0 144.8 jit_solution(5852264955116125852)
XLA Ops:
  1.3 141.1 %shard_map.77 = (bf16[128,32,128]{2,1,0:T(8,128)(2,1)}, bf16[128,32,128]{2,1,0:T(8,128)(2,1)}) custom-call(bf16[768,512]{1,0:T(8,128)(2,1)} %tokens_ref.1, bf16[768,512]{1,0:T(8,128)(2,1)} %grad_ref.1, bf16[128,128,128]{2,1,0:T(8,128)(2,1)} %w_in_ref.1, bf16[128,128,128]{2,1,0:T(8,128)(2,1)} %w_out_ref.1, s32[128]{0:T(128)} %ids_ref.1, s32[1]{0:T(128)S(6)} %copy.8.len_ref), custom_call_target="tpu_custom_call" | custom-call | tf_op jit(solution)/shard_map/pallas_call | solution.py:459
  142.4 2.4 %shard_map.78 = (bf16[128,32,128]{2,1,0:T(8,128)(2,1)}, bf16[128,32,128]{2,1,0:T(8,128)(2,1)}) custom-call(bf16[128,32,128]{2,1,0:T(8,128)(2,1)} %get-tuple-element.4.in_ref, bf16[128,32,128]{2,1,0:T(8,128)(2,1)} %get-tuple-element.5.out_ref), custom_call_target="tpu_custom_call" | custom-call | tf_op jit(solution)/shard_map/pallas_call | solution.py:496

commit v4 on v3

--- a/solution.py
+++ b/solution.py
@@ -71,18 +71,24 @@
 def pack_gather_grad_kernel(
     tokens_ref, grad_ref, w_in_ref, w_out_ref, ids_ref, len_ref, out_in_ref, out_out_ref,
     chip, lens, give, got, feat, w_in, w_out, part, from_core, to_x, from_x, staged,
+    feat_shared, part_shared, shared_core,
     load_sem, core_send, core_recv, x_send, x_recv, z_send, z_recv, y_send, y_recv,
     sum_core_send, sum_core_recv, sum_x_send, sum_x_recv, store_sem,
+    sz_send, sz_recv, sy_send, sy_recv, sx_send, sx_recv, sc_send, sc_recv,
 ):
     rows = chip.shape[2]
     width = chip.shape[3]
-    keep = feat.shape[1]
+    solo = feat.shape[1]
+    origin = feat_shared.shape[2]
+    keep = solo + origin
     spare = got.shape[1]
     per = width // BLOCK_SIDE
     n_rows = feat.shape[0] // 2
     groups = part.shape[1]
     pieces = 2 * per
     early = rows - 2 * spare
+    head = 2 * early
+    halves = (pl.ds(0, head), pl.ds(head, rows - head))
 
     blk = lax.axis_index("blk")
     seq = lax.axis_index("seq")
@@ -125,38 +131,48 @@
     lens[core] = jnp.full(lens.shape[1:], len_ref[0], jnp.int32)
     pl.semaphore_wait(barrier, 3 + jnp.where(z > 0, 1, 0) + jnp.where(z < NZ - 1, 1, 0))
 
-    len_swap = remote(lens.at[core], lens.at[core], core_send.at[2], core_recv.at[2], core_dev)
+    len_swap = remote(lens.at[core], lens.at[core], core_send.at[4], core_recv.at[4], core_dev)
     len_swap.start()
     swaps = [
-        remote(ref, chip.at[a, core], core_send.at[a], core_recv.at[a], core_dev)
-        for a, ref in enumerate((tokens_ref, grad_ref))
+        [
+            remote(
+                ref.at[half], chip.at[a, core, half],
+                core_send.at[2 * h + a], core_recv.at[2 * h + a], core_dev,
+            )
+            for a, ref in enumerate((tokens_ref, grad_ref))
+        ]
+        for h, half in enumerate(halves)
     ]
-    for swap in swaps:
+    for swap in swaps[0] + swaps[1]:
         swap.start()
     len_swap.wait()
     len_a = lens[0][0:1, 0:1]
     len_b = lens[1][0:1, 0:1]
     count = len_a + len_b
-    row = lax.broadcasted_iota(jnp.int32, (1, 2 * rows), 1)
-    place = jnp.where(
-        row < rows,
-        jnp.where(row < len_a, row, -1),
-        jnp.where(row - rows < len_b, row - rows + len_a, -1),
-    )
+
+    def places(held):
+        row = lax.broadcasted_iota(jnp.int32, (1, 2 * held), 1)
+        return jnp.where(
+            row < held,
+            jnp.where(row < len_a, row, -1),
+            jnp.where(row - held < len_b, row - held + len_a, -1),
+        )
+
+    place = places(rows)
     odd_give = jnp.bitwise_and(4 * keep - count + core, 1)
     odd_got = jnp.bitwise_and(count + core, 1)
     keep_at = 2 * lax.broadcasted_iota(jnp.int32, (keep, 1), 0) + core
     give_at = 2 * keep + odd_give + 2 * lax.broadcasted_iota(jnp.int32, (spare, 1), 0)
     got_at = count + odd_got + 2 * lax.broadcasted_iota(jnp.int32, (1, spare), 1)
     one, zero = jnp.float32(1), jnp.float32(0)
-    pick_early = jnp.where(place == keep_at[:early], one, zero).astype(jnp.bfloat16)
+    pick_early = jnp.where(places(head) == keep_at[:early], one, zero).astype(jnp.bfloat16)
     pick_late = jnp.where(place == keep_at[early:], one, zero).astype(jnp.bfloat16)
     pick_give = jnp.where(place == give_at, one, zero).astype(jnp.bfloat16)
     pick_got = jnp.where(got_at == keep_at[early:], one, zero).astype(jnp.bfloat16)
 
     def feat_piece(source, late, p):
         at = feat.at[(p // per) * n_rows + per * source + p % per]
-        return at.at[pl.ds(early, keep - early)] if late else at.at[pl.ds(0, early)]
+        return at.at[pl.ds(early, solo - early)] if late else at.at[pl.ds(0, early)]
 
     def z_copy(up, source_z, other, late, p, recv_only=False):
         ref = feat_piece(2 * source_z + (1 - y if other else y), late, p)
@@ -238,15 +254,75 @@
                 :, i * BLOCK_SIDE : (i + 1) * BLOCK_SIDE
             ]
 
+    def share_x(a):
+        ref = feat_shared.at[pl.ds(a * n_rows + per * blk, per), x]
+        return remote(ref, ref, sx_send.at[a], sx_recv.at[a], x_dev)
+
+    def shared_piece(source, p):
+        return feat_shared.at[(p // per) * n_rows + per * source + p % per]
+
+    def shared_z(up, source_z, p, recv_only=False):
+        ref = shared_piece(2 * source_z + y, p)
+        return remote(
+            ref, ref, sz_send.at[0 if up else 1, source_z, p], sz_recv.at[source_z, p],
+            y_dev if recv_only else (up_dev if up else down_dev),
+        )
+
+    def shared_y(source_z, source_y, p):
+        ref = shared_piece(2 * source_z + source_y, p)
+        return remote(ref, ref, sy_send.at[source_z, p], sy_recv.at[source_z, p], y_dev)
+
+    def send_shared(p, carry):
+        shared_y(z, y, p).start()
+
+        @pl.when(z < NZ - 1)
+        def _():
+            shared_z(True, z, p).start()
+
+        @pl.when(z > 0)
+        def _():
+            shared_z(False, z, p).start()
+
+        return carry
+
+    def pass_shared(k, carry):
+        step, p = k // pieces, k % pieces
+        below = z - 1 - step
+        above = z + 1 + step
+
+        @pl.when(below >= 0)
+        def _():
+            shared_z(True, below, p, recv_only=True).wait_recv()
+
+            @pl.when(z < NZ - 1)
+            def _():
+                shared_z(True, below, p).start()
+
+            shared_y(below, y, p).start()
+
+        @pl.when(above < NZ)
+        def _():
+            shared_z(False, above, p, recv_only=True).wait_recv()
+
+            @pl.when(z > 0)
+            def _():
+                shared_z(False, above, p).start()
+
+            shared_y(above, y, p).start()
+
+        return carry
+
     for a in range(2):
         own_loads[a].wait()
-        swaps[a].wait()
-        place_block(jnp.dot(pick_early, both(a), preferred_element_type=jnp.float32), 0, a)
+        swaps[0][a].wait()
+        heads = chip[a, :, :head].reshape(2 * head, width)
+        place_block(jnp.dot(pick_early, heads, preferred_element_type=jnp.float32), 0, a)
         send_own(False, a)
     for load in weight_loads:
         load.start()
     x_moves = []
     for a in range(2):
+        swaps[1][a].wait()
         give[a] = jnp.dot(pick_give, both(a), preferred_element_type=jnp.float32).astype(jnp.bfloat16)
         move = remote(give.at[a], got.at[a], x_send.at[a], x_recv.at[a], x_dev)
         move.start()
@@ -262,13 +338,23 @@
     for a in range(2):
         kept = jnp.dot(pick_late, both(a), preferred_element_type=jnp.float32)
         x_moves[a].wait()
-        place_block(kept + jnp.dot(pick_got, got[a], preferred_element_type=jnp.float32), early, a)
+        kept = kept + jnp.dot(pick_got, got[a], preferred_element_type=jnp.float32)
+        place_block(kept[: solo - early], early, a)
         send_own(True, a)
+        last = kept[solo - early :].astype(jnp.bfloat16)
+        for i in range(per):
+            feat_shared[a * n_rows + per * blk + i, x] = last[
+                :, i * BLOCK_SIDE : (i + 1) * BLOCK_SIDE
+            ]
+        share_x(a).start()
     pass_on(1, False)
     pass_on(0, True)
     pass_on(2, False)
     pass_on(1, True)
     pass_on(2, True)
+    for a in range(2):
+        share_x(a).wait()
+    lax.fori_loop(0, pieces, send_shared, 0)
 
     def end_early(p, carry):
         for source_z in range(NZ):
@@ -312,10 +398,10 @@
     quarter = BLOCK_SIDE // 4
     first = (((0,), (0,)), ((), ()))
 
-    def column_inputs(g):
+    def column_inputs(g, rows_of):
         ids = [ids_ref[BLOCKS_PER_COLUMN * g + i] for i in range(BLOCKS_PER_COLUMN)]
-        x_cat = jnp.concatenate([feat[r] for r in ids], axis=1)
-        g_cat = jnp.concatenate([feat[n_rows + r] for r in ids], axis=1)
+        x_cat = jnp.concatenate([rows_of(r) for r in ids], axis=1)
+        g_cat = jnp.concatenate([rows_of(n_rows + r) for r in ids], axis=1)
         slots = pl.ds(BLOCKS_PER_COLUMN * g, BLOCKS_PER_COLUMN)
         w_rows = w_in[slots].reshape(BLOCKS_PER_COLUMN * BLOCK_SIDE, BLOCK_SIDE)
         wo = w_out[slots]
@@ -326,7 +412,7 @@
         )
         return x_cat, g_cat, pre_act, grad_act
 
-    def column_grads(g, x_cat, g_cat, pre_act, grad_act):
+    def column_grads(store, g, x_cat, g_cat, pre_act, grad_act):
         activation, gelu_slope = gelu_pair(pre_act)
         activation = activation.astype(jnp.bfloat16)
         grad_pre = (grad_act * gelu_slope).astype(jnp.bfloat16)
@@ -339,14 +425,32 @@
             two = (share_in[:, cols].T, share_out[:, cols])
             for a in range(2):
                 for q in range(4):
-                    part[q % 2, g, q // 2, a, i] = two[a][q * quarter : (q + 1) * quarter]
+                    store(q % 2, q // 2, g, a, i, two[a][q * quarter : (q + 1) * quarter])
+
+    def columns_of(t, rows_of, store):
+        columns = [TOGETHER * t + u for u in range(TOGETHER)]
+        held = [column_inputs(g, rows_of) for g in columns]
+        for g, values in zip(columns, held):
+            column_grads(store, g, *values)
+
+    def solo_rows(r):
+        return feat[r]
+
+    def solo_store(to_core, to_chip, g, a, i, value):
+        part[to_core, g, to_chip, a, i] = value
+
+    def shared_rows(r):
+        return feat_shared[r].reshape(2 * origin, BLOCK_SIDE)
+
+    def shared_store(to_core, to_chip, g, a, i, value):
+        part_shared[to_core, to_chip, g, a, i] = value
+
+    n_pass = (NZ - 1) * pieces
 
     def turn_columns(t, carry):
-        columns = [TOGETHER * t + u for u in range(TOGETHER)]
-        held = [column_inputs(g) for g in columns]
-        for g, values in zip(columns, held):
-            column_grads(g, *values)
+        columns_of(t, solo_rows, solo_store)
         core_sum(t).start()
+        lax.fori_loop(n_pass * t // turns, n_pass * (t + 1) // turns, pass_shared, 0)
 
         @pl.when(t > 0)
         def _():
@@ -356,6 +460,19 @@
 
     lax.fori_loop(0, turns, turn_columns, 0)
     send_sum(turns - 1)
+
+    def end_shared(p, carry):
+        for source_z in range(NZ):
+            shared_y(source_z, 1 - y, p).wait_recv()
+        return carry
+
+    lax.fori_loop(0, pieces, end_shared, 0)
+
+    def shared_sum(t):
+        return remote(
+            part_shared.at[1 - core, x, span(t)], shared_core.at[span(t)],
+            sc_send.at[t], sc_recv.at[t], core_dev,
+        )
 
     per_turn = TOGETHER * BLOCKS_PER_COLUMN
 
@@ -366,12 +483,15 @@
             for a, ref in enumerate((out_in_ref, out_out_ref))
         ]
 
-    def finish(t, carry):
+    def finish(t):
+        shared_sum(t).wait_recv()
         x_sum(t).wait_recv()
         total = (
             part[core, span(t), x].astype(jnp.float32)
             + from_core[span(t), x].astype(jnp.float32)
             + from_x[span(t)].astype(jnp.float32)
+            + part_shared[core, x, span(t)].astype(jnp.float32)
+            + shared_core[span(t)].astype(jnp.float32)
         ).astype(jnp.bfloat16)
         for u in range(TOGETHER):
             at = pl.ds(per_turn * t + u * BLOCKS_PER_COLUMN, BLOCKS_PER_COLUMN)
@@ -379,13 +499,24 @@
                 staged[a, at] = total[u, a]
         for store in stores(t):
             store.start()
-        return carry
-
-    lax.fori_loop(0, turns, finish, 0)
+
+    def turn_shared(t, carry):
+        columns_of(t, shared_rows, shared_store)
+        shared_sum(t).start()
+
+        @pl.when(t > 0)
+        def _():
+            finish(t - 1)
+
+        return carry
+
+    lax.fori_loop(0, turns, turn_shared, 0)
+    finish(turns - 1)
 
     def end_sums(t, carry):
         core_sum(t).wait_send()
         x_sum(t).wait_send()
+        shared_sum(t).wait_send()
         for store in stores(t):
             store.wait()
         return carry
@@ -419,6 +550,22 @@
     lax.fori_loop(ACROSS, pieces, end_sends(False, False, False), 0)
     lax.fori_loop(0, ACROSS, end_sends(True, False, True), 0)
     lax.fori_loop(0, pieces, end_sends(False, True, False), 0)
+
+    def end_shared_sends(p, carry):
+        for source_z in range(NZ):
+            shared_y(source_z, y, p).wait_send()
+
+            @pl.when(jnp.logical_and(z < NZ - 1, source_z <= z))
+            def _():
+                shared_z(True, source_z, p).wait_send()
+
+            @pl.when(jnp.logical_and(z > 0, source_z >= z))
+            def _():
+                shared_z(False, source_z, p).wait_send()
+
+        return carry
+
+    lax.fori_loop(0, pieces, end_shared_sends, 0)
 
 
 def deliver_kernel(in_ref, out_ref, in_final, out_final, held, sems):
@@ -447,6 +594,9 @@
     n_blk, n_seq = PLAN_MESH
     keep = rows * 5 // 8
     spare = rows - keep
+    origin = keep // 5
+    solo = keep - origin
+    turns = groups // TOGETHER
     n_rows = n_blk * width // BLOCK_SIDE
     pieces = 2 * width // BLOCK_SIDE
     quarter = BLOCK_SIDE // n_seq
@@ -466,7 +616,7 @@
             pltpu.VMEM((2, 8, 128), jnp.int32),
             pltpu.VMEM((2, spare, width), bf16),
             pltpu.VMEM((2, spare, width), bf16),
-            pltpu.VMEM((2 * n_rows, keep, BLOCK_SIDE), bf16),
+            pltpu.VMEM((2 * n_rows, solo, BLOCK_SIDE), bf16),
             pltpu.VMEM((slots, BLOCK_SIDE, BLOCK_SIDE), bf16),
             pltpu.VMEM((slots, BLOCK_SIDE, BLOCK_SIDE), bf16),
             pltpu.VMEM((2, groups, 2) + sums, bf16),
@@ -474,23 +624,34 @@
             pltpu.VMEM((groups,) + sums, bf16),
             pltpu.VMEM((groups,) + sums, bf16),
             pltpu.VMEM((2, slots, quarter, BLOCK_SIDE), bf16),
+            pltpu.VMEM((2 * n_rows, 2, origin, BLOCK_SIDE), bf16),
+            pltpu.VMEM((2, 2, groups) + sums, bf16),
+            pltpu.VMEM((groups,) + sums, bf16),
             dma((4,)),
-            dma((3,)),
-            dma((3,)),
+            dma((5,)),
+            dma((5,)),
             dma((2,)),
             dma((2,)),
             dma((2, NZ, 2 * pieces + ACROSS)),
             dma((NZ, 2 * pieces + ACROSS)),
             dma((NZ, 2 * pieces)),
             dma((NZ, 2 * pieces)),
-            dma((groups // TOGETHER,)),
-            dma((groups // TOGETHER,)),
-            dma((groups // TOGETHER,)),
-            dma((groups // TOGETHER,)),
-            dma((2, groups // TOGETHER)),
+            dma((turns,)),
+            dma((turns,)),
+            dma((turns,)),
+            dma((turns,)),
+            dma((2, turns)),
+            dma((2, NZ, pieces)),
+            dma((NZ, pieces)),
+            dma((NZ, pieces)),
+            dma((NZ, pieces)),
+            dma((2,)),
+            dma((2,)),
+            dma((turns,)),
+            dma((turns,)),
         ],
         compiler_params=pltpu.CompilerParams(
-            collective_id=0, has_side_effects=True, vmem_limit_bytes=56 * 1024 * 1024
+            collective_id=0, has_side_effects=True, vmem_limit_bytes=60 * 1024 * 1024
         ),
     )(tokens, grad_out, input_weight_blocks, output_weight_blocks, row_ids, lengths)
     return pl.pallas_call(

time: 145 us -> 134 us (0.924)
  Pallas kernels: 143 us -> 132 us
    pallas_call x1, Pallas kernels: 141 us -> 130 us  [packed_shards(): pl.pallas_call(pack_gather_grad_kernel, out_shape=(out, out), in_specs=[a...]
where the time goes in v4:
time: 134 us
  Pallas kernels  132 us (99%)
    pallas_call x1, Pallas kernels, packed_shards(): pl.pallas_call(pack_gather_grad_kernel, out_shape=(out, out), in_specs=[a...  130 us

profile of v4, /device:TPU:0, one launch (start us, length us, event | category | flops | bytes accessed | tf_op | source)
XLA Modules:
  0.0 133.5 jit_solution(947452340245892371)
XLA Ops:
  1.3 129.8 %shard_map.77 = (bf16[128,32,128]{2,1,0:T(8,128)(2,1)}, bf16[128,32,128]{2,1,0:T(8,128)(2,1)}) custom-call(bf16[768,512]{1,0:T(8,128)(2,1)} %tokens_ref.1, bf16[768,512]{1,0:T(8,128)(2,1)} %grad_ref.1, bf16[128,128,128]{2,1,0:T(8,128)(2,1)} %w_in_ref.1, bf16[128,128,128]{2,1,0:T(8,128)(2,1)} %w_out_ref.1, s32[128]{0:T(128)} %ids_ref.1, s32[1]{0:T(128)S(6)} %copy.8.len_ref), custom_call_target="tpu_custom_call" | custom-call | tf_op jit(solution)/shard_map/pallas_call | solution.py:609
  131.1 2.4 %shard_map.78 = (bf16[128,32,128]{2,1,0:T(8,128)(2,1)}, bf16[128,32,128]{2,1,0:T(8,128)(2,1)}) custom-call(bf16[128,32,128]{2,1,0:T(8,128)(2,1)} %get-tuple-element.4.in_ref, bf16[128,32,128]{2,1,0:T(8,128)(2,1)} %get-tuple-element.5.out_ref), custom_call_target="tpu_custom_call" | custom-call | tf_op jit(solution)/shard_map/pallas_call | solution.py:657

commit v5 on v4

--- a/solution.py
+++ b/solution.py
@@ -71,7 +71,7 @@
 def pack_gather_grad_kernel(
     tokens_ref, grad_ref, w_in_ref, w_out_ref, ids_ref, len_ref, out_in_ref, out_out_ref,
     chip, lens, give, got, feat, w_in, w_out, part, from_core, to_x, from_x, staged,
-    feat_shared, part_shared, shared_core,
+    feat_shared, part_shared, shared_core, mid,
     load_sem, core_send, core_recv, x_send, x_recv, z_send, z_recv, y_send, y_recv,
     sum_core_send, sum_core_recv, sum_x_send, sum_x_recv, store_sem,
     sz_send, sz_recv, sy_send, sy_recv, sx_send, sx_recv, sc_send, sc_recv,
@@ -205,7 +205,7 @@
 
         lax.fori_loop(0, per, body, 0)
 
-    def pass_on(step, late):
+    def pass_on(step, late, own=True, others=True):
         below = z - 1 - step
         above = z + 1 + step
 
@@ -239,9 +239,10 @@
 
         if late:
             lax.fori_loop(0, pieces, arrivals(False, False), 0)
-        else:
+        if own and not late:
             lax.fori_loop(0, ACROSS, arrivals(False, True), 0)
             lax.fori_loop(ACROSS, pieces, arrivals(False, False), 0)
+        if others and not late:
             lax.fori_loop(0, ACROSS, arrivals(True, True), 0)
 
     def both(a):
@@ -327,6 +328,8 @@
         move = remote(give.at[a], got.at[a], x_send.at[a], x_recv.at[a], x_dev)
         move.start()
         x_moves.append(move)
+    for a in range(2):
+        mid[a] = jnp.dot(pick_late, both(a), preferred_element_type=jnp.float32).astype(jnp.bfloat16)
 
     def turn(p, carry):
         y_copy(z, 1 - y, False, p).wait_recv()
@@ -335,10 +338,10 @@
 
     lax.fori_loop(0, ACROSS, turn, 0)
     pass_on(0, False)
+    pass_on(1, False, others=False)
     for a in range(2):
-        kept = jnp.dot(pick_late, both(a), preferred_element_type=jnp.float32)
         x_moves[a].wait()
-        kept = kept + jnp.dot(pick_got, got[a], preferred_element_type=jnp.float32)
+        kept = mid[a].astype(jnp.float32) + jnp.dot(pick_got, got[a], preferred_element_type=jnp.float32)
         place_block(kept[: solo - early], early, a)
         send_own(True, a)
         last = kept[solo - early :].astype(jnp.bfloat16)
@@ -347,7 +350,7 @@
                 :, i * BLOCK_SIDE : (i + 1) * BLOCK_SIDE
             ]
         share_x(a).start()
-    pass_on(1, False)
+    pass_on(1, False, own=False)
     pass_on(0, True)
     pass_on(2, False)
     pass_on(1, True)
@@ -372,28 +375,24 @@
     for load in weight_loads:
         load.wait()
 
+    def core_sum(g):
+        return remote(
+            part.at[1 - core, g], from_core.at[g], sum_core_send.at[g], sum_core_recv.at[g], core_dev
+        )
+
+    def x_sum(g):
+        return remote(to_x.at[g], from_x.at[g], sum_x_send.at[g], sum_x_recv.at[g], x_dev)
+
+    def send_sum(g):
+        core_sum(g).wait_recv()
+        total = part[core, g, 1 - x].astype(jnp.float32) + from_core[g, 1 - x].astype(jnp.float32)
+        to_x[g] = total.astype(jnp.bfloat16)
+        x_sum(g).start()
+
     turns = groups // TOGETHER
 
     def span(t):
         return pl.ds(TOGETHER * t, TOGETHER)
-
-    def core_sum(t):
-        return remote(
-            part.at[1 - core, span(t)], from_core.at[span(t)],
-            sum_core_send.at[t], sum_core_recv.at[t], core_dev,
-        )
-
-    def x_sum(t):
-        return remote(
-            to_x.at[span(t)], from_x.at[span(t)], sum_x_send.at[t], sum_x_recv.at[t], x_dev
-        )
-
-    def send_sum(t):
-        core_sum(t).wait_recv()
-        total = part[core, span(t), 1 - x].astype(jnp.float32)
-        total = total + from_core[span(t), 1 - x].astype(jnp.float32)
-        to_x[span(t)] = total.astype(jnp.bfloat16)
-        x_sum(t).start()
 
     quarter = BLOCK_SIDE // 4
     first = (((0,), (0,)), ((), ()))
@@ -427,8 +426,7 @@
                 for q in range(4):
                     store(q % 2, q // 2, g, a, i, two[a][q * quarter : (q + 1) * quarter])
 
-    def columns_of(t, rows_of, store):
-        columns = [TOGETHER * t + u for u in range(TOGETHER)]
+    def columns_of(columns, rows_of, store):
         held = [column_inputs(g, rows_of) for g in columns]
         for g, values in zip(columns, held):
             column_grads(store, g, *values)
@@ -447,19 +445,19 @@
 
     n_pass = (NZ - 1) * pieces
 
-    def turn_columns(t, carry):
-        columns_of(t, solo_rows, solo_store)
-        core_sum(t).start()
-        lax.fori_loop(n_pass * t // turns, n_pass * (t + 1) // turns, pass_shared, 0)
-
-        @pl.when(t > 0)
-        def _():
-            send_sum(t - 1)
-
-        return carry
-
-    lax.fori_loop(0, turns, turn_columns, 0)
-    send_sum(turns - 1)
+    def solo_column(g, carry):
+        columns_of([g], solo_rows, solo_store)
+        core_sum(g).start()
+
+        @pl.when(g > 0)
+        def _():
+            send_sum(g - 1)
+
+        lax.fori_loop(n_pass * g // groups, n_pass * (g + 1) // groups, pass_shared, 0)
+        return carry
+
+    lax.fori_loop(0, groups, solo_column, 0)
+    send_sum(groups - 1)
 
     def end_shared(p, carry):
         for source_z in range(NZ):
@@ -485,7 +483,8 @@
 
     def finish(t):
         shared_sum(t).wait_recv()
-        x_sum(t).wait_recv()
+        for u in range(TOGETHER):
+            x_sum(TOGETHER * t + u).wait_recv()
         total = (
             part[core, span(t), x].astype(jnp.float32)
             + from_core[span(t), x].astype(jnp.float32)
@@ -501,7 +500,7 @@
             store.start()
 
     def turn_shared(t, carry):
-        columns_of(t, shared_rows, shared_store)
+        columns_of([TOGETHER * t + u for u in range(TOGETHER)], shared_rows, shared_store)
         shared_sum(t).start()
 
         @pl.when(t > 0)
@@ -514,8 +513,9 @@
     finish(turns - 1)
 
     def end_sums(t, carry):
-        core_sum(t).wait_send()
-        x_sum(t).wait_send()
+        for u in range(TOGETHER):
+            core_sum(TOGETHER * t + u).wait_send()
+            x_sum(TOGETHER * t + u).wait_send()
         shared_sum(t).wait_send()
         for store in stores(t):
             store.wait()
@@ -627,6 +627,7 @@
             pltpu.VMEM((2 * n_rows, 2, origin, BLOCK_SIDE), bf16),
             pltpu.VMEM((2, 2, groups) + sums, bf16),
             pltpu.VMEM((groups,) + sums, bf16),
+            pltpu.VMEM((2, spare, width), bf16),
             dma((4,)),
             dma((5,)),
             dma((5,)),
@@ -636,10 +637,10 @@
             dma((NZ, 2 * pieces + ACROSS)),
             dma((NZ, 2 * pieces)),
             dma((NZ, 2 * pieces)),
-            dma((turns,)),
-            dma((turns,)),
-            dma((turns,)),
-            dma((turns,)),
+            dma((groups,)),
+            dma((groups,)),
+            dma((groups,)),
+            dma((groups,)),
             dma((2, turns)),
             dma((2, NZ, pieces)),
             dma((NZ, pieces)),

time: 134 us -> 136 us (1.015)
  Pallas kernels: 132 us -> 134 us
    pallas_call x1, Pallas kernels: 130 us -> 132 us  [packed_shards(): pl.pallas_call(pack_gather_grad_kernel, out_shape=(out, out), in_specs=[a...]
where the time goes in v5:
time: 136 us
  Pallas kernels  134 us (99%)
    pallas_call x1, Pallas kernels, packed_shards(): pl.pallas_call(pack_gather_grad_kernel, out_shape=(out, out), in_specs=[a...  132 us

profile of v5, /device:TPU:0, one launch (start us, length us, event | category | flops | bytes accessed | tf_op | source)
XLA Modules:
  0.0 135.8 jit_solution(15651220210462823115)
XLA Ops:
  1.3 132.1 %shard_map.77 = (bf16[128,32,128]{2,1,0:T(8,128)(2,1)}, bf16[128,32,128]{2,1,0:T(8,128)(2,1)}) custom-call(bf16[768,512]{1,0:T(8,128)(2,1)} %tokens_ref.1, bf16[768,512]{1,0:T(8,128)(2,1)} %grad_ref.1, bf16[128,128,128]{2,1,0:T(8,128)(2,1)} %w_in_ref.1, bf16[128,128,128]{2,1,0:T(8,128)(2,1)} %w_out_ref.1, s32[128]{0:T(128)} %ids_ref.1, s32[1]{0:T(128)S(6)} %copy.8.len_ref), custom_call_target="tpu_custom_call" | custom-call | tf_op jit(solution)/shard_map/pallas_call | solution.py:609
  133.4 2.4 %shard_map.78 = (bf16[128,32,128]{2,1,0:T(8,128)(2,1)}, bf16[128,32,128]{2,1,0:T(8,128)(2,1)}) custom-call(bf16[128,32,128]{2,1,0:T(8,128)(2,1)} %get-tuple-element.4.in_ref, bf16[128,32,128]{2,1,0:T(8,128)(2,1)} %get-tuple-element.5.out_ref), custom_call_target="tpu_custom_call" | custom-call | tf_op jit(solution)/shard_map/pallas_call | solution.py:658

commit v6 on v5

--- a/solution.py
+++ b/solution.py
@@ -63,7 +63,8 @@
 PLAN_MESH = (8, 4)
 NZ = 4
 ACROSS = 3
-TOGETHER = 2
+SOLO_TOGETHER = 2
+TOGETHER = 4
 DELIVERY_PARTS = 4
 MESH = pl.DeviceIdType.MESH
 
@@ -445,19 +446,25 @@
 
     n_pass = (NZ - 1) * pieces
 
-    def solo_column(g, carry):
-        columns_of([g], solo_rows, solo_store)
-        core_sum(g).start()
-
-        @pl.when(g > 0)
-        def _():
-            send_sum(g - 1)
-
-        lax.fori_loop(n_pass * g // groups, n_pass * (g + 1) // groups, pass_shared, 0)
-        return carry
-
-    lax.fori_loop(0, groups, solo_column, 0)
-    send_sum(groups - 1)
+    solo_turns = groups // SOLO_TOGETHER
+
+    def solo_columns(t, carry):
+        columns = [SOLO_TOGETHER * t + u for u in range(SOLO_TOGETHER)]
+        columns_of(columns, solo_rows, solo_store)
+        for g in columns:
+            core_sum(g).start()
+
+        @pl.when(t > 0)
+        def _():
+            for g in columns:
+                send_sum(g - SOLO_TOGETHER)
+
+        lax.fori_loop(n_pass * t // solo_turns, n_pass * (t + 1) // solo_turns, pass_shared, 0)
+        return carry
+
+    lax.fori_loop(0, solo_turns, solo_columns, 0)
+    for u in range(SOLO_TOGETHER):
+        send_sum(groups - SOLO_TOGETHER + u)
 
     def end_shared(p, carry):
         for source_z in range(NZ):

time: 136 us -> 136 us (level)
  no operation moved by 1% of the time
where the time goes in v6:
time: 136 us
  Pallas kernels  135 us (99%)
    pallas_call x1, Pallas kernels, packed_shards(): pl.pallas_call(pack_gather_grad_kernel, out_shape=(out, out), in_specs=[a...  132 us

profile of v6, /device:TPU:0, one launch (start us, length us, event | category | flops | bytes accessed | tf_op | source)
XLA Modules:
  0.0 135.9 jit_solution(9765141504142350992)
XLA Ops:
  1.3 132.2 %shard_map.77 = (bf16[128,32,128]{2,1,0:T(8,128)(2,1)}, bf16[128,32,128]{2,1,0:T(8,128)(2,1)}) custom-call(bf16[768,512]{1,0:T(8,128)(2,1)} %tokens_ref.1, bf16[768,512]{1,0:T(8,128)(2,1)} %grad_ref.1, bf16[128,128,128]{2,1,0:T(8,128)(2,1)} %w_in_ref.1, bf16[128,128,128]{2,1,0:T(8,128)(2,1)} %w_out_ref.1, s32[128]{0:T(128)} %ids_ref.1, s32[1]{0:T(128)S(6)} %copy.8.len_ref), custom_call_target="tpu_custom_call" | custom-call | tf_op jit(solution)/shard_map/pallas_call | solution.py:616
  133.5 2.4 %shard_map.78 = (bf16[128,32,128]{2,1,0:T(8,128)(2,1)}, bf16[128,32,128]{2,1,0:T(8,128)(2,1)}) custom-call(bf16[128,32,128]{2,1,0:T(8,128)(2,1)} %get-tuple-element.4.in_ref, bf16[128,32,128]{2,1,0:T(8,128)(2,1)} %get-tuple-element.5.out_ref), custom_call_target="tpu_custom_call" | custom-call | tf_op jit(solution)/shard_map/pallas_call | solution.py:665

commit v7 on v6

--- a/solution.py
+++ b/solution.py
@@ -339,7 +339,6 @@
 
     lax.fori_loop(0, ACROSS, turn, 0)
     pass_on(0, False)
-    pass_on(1, False, others=False)
     for a in range(2):
         x_moves[a].wait()
         kept = mid[a].astype(jnp.float32) + jnp.dot(pick_got, got[a], preferred_element_type=jnp.float32)
@@ -351,7 +350,7 @@
                 :, i * BLOCK_SIDE : (i + 1) * BLOCK_SIDE
             ]
         share_x(a).start()
-    pass_on(1, False, own=False)
+    pass_on(1, False)
     pass_on(0, True)
     pass_on(2, False)
     pass_on(1, True)
@@ -601,7 +600,7 @@
     n_blk, n_seq = PLAN_MESH
     keep = rows * 5 // 8
     spare = rows - keep
-    origin = keep // 5
+    origin = keep * 7 // 30
     solo = keep - origin
     turns = groups // TOGETHER
     n_rows = n_blk * width // BLOCK_SIDE

time: 136 us -> 132 us (0.971)
  Pallas kernels: 135 us -> 130 us
    pallas_call x1, Pallas kernels: 132 us -> 128 us  [packed_shards(): pl.pallas_call(pack_gather_grad_kernel, out_shape=(out, out), in_specs=[a...]
where the time goes in v7:
time: 132 us
  Pallas kernels  130 us (98%)
    pallas_call x1, Pallas kernels, packed_shards(): pl.pallas_call(pack_gather_grad_kernel, out_shape=(out, out), in_specs=[a...  128 us

profile of v7, /device:TPU:0, one launch (start us, length us, event | category | flops | bytes accessed | tf_op | source)
XLA Modules:
  0.0 131.6 jit_solution(17059791620531392967)
XLA Ops:
  1.3 127.9 %shard_map.77 = (bf16[128,32,128]{2,1,0:T(8,128)(2,1)}, bf16[128,32,128]{2,1,0:T(8,128)(2,1)}) custom-call(bf16[768,512]{1,0:T(8,128)(2,1)} %tokens_ref.1, bf16[768,512]{1,0:T(8,128)(2,1)} %grad_ref.1, bf16[128,128,128]{2,1,0:T(8,128)(2,1)} %w_in_ref.1, bf16[128,128,128]{2,1,0:T(8,128)(2,1)} %w_out_ref.1, s32[128]{0:T(128)} %ids_ref.1, s32[1]{0:T(128)S(6)} %copy.8.len_ref), custom_call_target="tpu_custom_call" | custom-call | tf_op jit(solution)/shard_map/pallas_call | solution.py:615
  129.2 2.4 %shard_map.78 = (bf16[128,32,128]{2,1,0:T(8,128)(2,1)}, bf16[128,32,128]{2,1,0:T(8,128)(2,1)}) custom-call(bf16[128,32,128]{2,1,0:T(8,128)(2,1)} %get-tuple-element.4.in_ref, bf16[128,32,128]{2,1,0:T(8,128)(2,1)} %get-tuple-element.5.out_ref), custom_call_target="tpu_custom_call" | custom-call | tf_op jit(solution)/shard_map/pallas_call | solution.py:664
